TPU v7x, 32 devices: a whole 2x2x4 slice. The times are simulated.
32 devices in a mesh: groups: 2 (over y), expert: 8 (over z, core), split: 2 (over x).
Axes of the slice: x: 2, y: 2, z: 4, core: 2. Of those that a mesh axis runs over, the one named last changes fastest.
Arguments:
- tokens: bfloat16 [512, 3584], P(('groups', 'expert', 'split')), parts along dimension 0, may hold values from -6 to 6
- expert_ids: int32 [512, 8], P(('groups', 'expert', 'split')), parts along dimension 0, may hold values from 0 to 15, all different within a row; in each aligned block of 16 rows (0 to 15, 16 to 31, ...) at most 8 rows name the same one
- gate_weights: float32 [512, 8], P(('groups', 'expert', 'split')), parts along dimension 0, may hold values from 0.1 to 0.5
- w_gate: bfloat16 [16, 3584, 1024], P('expert', None, 'split'), may hold values from -0.09375 to 0.09375
- w_up: bfloat16 [16, 3584, 1024], P('expert', None, 'split'), may hold values from -0.09375 to 0.09375
- w_down: bfloat16 [16, 1024, 3584], P('expert', 'split'), may hold values from -0.1875 to 0.1875
Outputs:
- mixed: bfloat16 [512, 3584], P(('groups', 'expert', 'split')), parts along dimension 0
There are 2 independent parts, one for each index of `groups`. A program takes and returns all parts, laid end to end along the dimension named above; an argument that names none is the same for every part. Nothing has to cross between parts.
Inputs may be any that keep to these rules, and one draw needn't show every extreme that they name: `expert_ids`: each token names 8 different experts. Within the rows of one device no expert is named by more than 8 tokens, and in every draw some device has an expert named by exactly 8 of its tokens.
All inputs are finite; a program needn't handle non-finite values.
Results may differ from a plain program's by a relative error of at most 0.0065.
Values may be sent and summed in bfloat16 or wider, within the bound.
A program may use at most 64 MiB of HBM per device.

v0:
```python
import jax
import jax.numpy as jnp
from jax import lax
from jax.sharding import PartitionSpec as P


def slot_targets(chosen_ids, capacity, expert_total):
    flat_ids = chosen_ids.reshape(-1)
    chosen = (flat_ids[:, None] == jnp.arange(expert_total, dtype=jnp.int32)[None, :]).astype(
        jnp.int32
    )
    earlier = jnp.cumsum(chosen, axis=0) - chosen
    slot_index = jnp.sum(earlier * chosen, axis=1)
    return (flat_ids * capacity + slot_index).reshape(chosen_ids.shape)


def shards(tokens, expert_ids, gate_weights, w_gate, w_up, w_down):
    expert_count = lax.axis_size("expert")
    local_count = w_gate.shape[0]
    expert_total = local_count * expert_count
    width = tokens.shape[1]
    capacity = max(3, tokens.shape[0] * expert_ids.shape[1] // expert_total)
    destination = slot_targets(expert_ids, capacity, expert_total)
    slot_range = jnp.arange(expert_total * capacity, dtype=jnp.int32)
    matches = slot_range[:, None, None] == destination[None, :, :]
    selector = jnp.any(matches, axis=-1).astype(jnp.bfloat16)
    send_buffer = jnp.dot(selector, tokens, preferred_element_type=jnp.float32).astype(jnp.bfloat16)
    send_buffer = send_buffer.reshape(expert_total, capacity, width)

    def run_experts(piece, start=0):
        block_shape = piece.shape
        row_block = piece.reshape(-1, local_count, capacity, width)
        gate_act = jnp.einsum(
            "mjcd,jdf->mjcf", row_block, w_gate, preferred_element_type=jnp.float32
        )
        up_act = jnp.einsum("mjcd,jdf->mjcf", row_block, w_up, preferred_element_type=jnp.float32)
        hidden = (jax.nn.silu(gate_act) * up_act).astype(jnp.bfloat16)
        partial_value = jnp.einsum(
            "mjcf,jfd->mjcd", hidden, w_down, preferred_element_type=jnp.float32
        )
        return partial_value.astype(jnp.bfloat16).reshape(block_shape)

    arrived = lax.all_to_all(send_buffer, "expert", split_axis=0, concat_axis=0, tiled=True)
    arrived = arrived.reshape(expert_count, 1, local_count, capacity, width)
    partial_value = run_experts(lax.all_gather(arrived, "split", axis=1, tiled=True), jnp.int32(0))
    summed = lax.psum_scatter(
        partial_value.astype(jnp.float32).astype(jnp.bfloat16),
        "split",
        scatter_dimension=1,
        tiled=True,
    )
    expert_out = summed.reshape(expert_total, capacity, width)
    returned = lax.all_to_all(expert_out, "expert", split_axis=0, concat_axis=0, tiled=True)
    combiner = jnp.sum(jnp.where(matches, gate_weights[None, :, :], 0.0), axis=-1).T
    mixed = jnp.dot(
        combiner,
        returned.reshape(expert_total * capacity, width).astype(jnp.float32),
        precision=lax.Precision.HIGHEST,
        preferred_element_type=jnp.float32,
    )
    return mixed.astype(jnp.bfloat16)


def solution(mesh):
    in_specs = (
        P(("groups", "expert", "split"), None),
        P(("groups", "expert", "split"), None),
        P(("groups", "expert", "split"), None),
        P("expert", None, "split"),
        P("expert", None, "split"),
        P("expert", "split", None),
    )
    out_specs = P(("groups", "expert", "split"), None)
    return jax.shard_map(shards, mesh=mesh, in_specs=in_specs, out_specs=out_specs, check_vma=False)
```

profile of v0, /device:TPU:0, one launch (start us, length us, event | category | flops | bytes accessed | tf_op | source)
XLA Modules:
  0.0 150.6 jit_solution(790479251284754370)
XLA Ops:
  6.5 0.0 copy-start
  6.5 0.0 all-gather.2.cloned.1.call-start
  6.5 0.8 copy.16
  7.3 0.1 eq.29
  7.4 0.1 fusion.31
  7.5 0.2 reduce_window_sum.11
  7.7 0.2 select_reduce_fusion.1
  7.9 0.1 reduce_sum.21
  8.0 0.1 fusion.32
  8.1 0.0 copy-done
  8.1 0.4 fusion.9
  8.5 29.9 %all_to_all.10 = bf16[16,8,3584]{2,1,0:T(8,128)(2,1)S(1)} all-to-all(bf16[16,8,3584]{2,1,0:T(8,128)(2,1)S(1)} %fusion.9), channel_id=1, replica_groups=mesh['groups'=2,'expert'=8,'split'=2] {'expert'}, dimensions={0} | all-to-all | bytes 1835008 | tf_op jit(solution)/shard_map/all_to_all | solution.py:43
  38.5 1.0 copy.19
  39.4 0.0 all-gather.2.cloned.1.call-update
  39.5 0.0 reduce-scatter.2.cloned.1.call-start
  39.5 29.2 %all-gather.2.cloned.1.call-done = bf16[8,2,2,8,3584]{4,3,1,0,2:T(8,128)(2,1)} async-done(((bf16[8,1,2,8,3584]{4,3,1,0,2:T(8,128)(2,1)}), bf16[8,2,2,8,3584]{4,3,1,0,2:T(8,128)(2,1)}) %all-gather.2.cloned.1.call-update) | async-done | bytes 1835024 | tf_op jit(solution)/shard_map/all_gather | solution.py:45
  68.7 0.0 copy-start.1
  68.7 4.9 %fusion.10 = f32[16,2,8,512]{3,2,0,1:T(8,128)S(1)} fusion(bf16[16,2,8,3584]{3,2,0,1:T(8,128)(2,1)} %bitcast.53, bf16[2,3584,512]{2,1,0:T(8,128)(2,1)} %param.9), kind=kOutput, calls=%fused_computation.10 | convolution fusion | flops 939524096 | bytes 9699328 | tf_op jit(solution)/shard_map/mjcd,jdf->mjcf/dot_general | solution.py:33
  73.6 0.0 copy-done.1
  73.6 8.5 %fusion.6 = bf16[2,16,8,3584]{3,2,1,0:T(8,128)(2,1)} fusion(bf16[2,512,3584]{2,1,0:T(8,128)(2,1)} %param.11, bf16[16,2,8,3584]{3,2,0,1:T(8,128)(2,1)S(1)} %bitcast.54, bf16[2,3584,512]{2,1,0:T(8,128)(2,1)} %param.10, f32[16,2,8,512]{3,2,0,1:T(8,128)S(1)} %fusion.10), kind=kOutput, calls=%fused_computation.6 | convolution fusion | flops 1880752128 | bytes 18874368 | tf_op jit(solution)/shard_map/mjcf,jfd->mjcd/dot_general | solution.py:38
  82.1 0.0 copy-start.2
  82.1 3.0 %copy.20 = bf16[8,2,2,8,3584]{4,3,2,0,1:T(8,128)(2,1)} copy(bf16[8,2,2,8,3584]{4,3,1,0,2:T(8,128)(2,1)} %bitcast.55) | data formatting | bytes 3670016 | tf_op jit(solution)/shard_map/reshape | solution.py:41
  85.1 0.0 reduce-scatter.2.cloned.1.call-update
  85.1 29.1 %reduce-scatter.2.cloned.1.call-done = bf16[8,1,2,8,3584]{4,3,2,0,1:T(8,128)(2,1)} async-done(((bf16[8,2,2,8,3584]{4,3,2,0,1:T(8,128)(2,1)}), bf16[8,1,2,8,3584]{4,3,2,0,1:T(8,128)(2,1)}) %reduce-scatter.2.cloned.1.call-update) | async-done | bytes 917520 | tf_op jit(solution)/shard_map/reduce_scatter | solution.py:46
  114.2 4.6 %all-to-all-start.1 = ((bf16[16,8,3584]{2,1,0:T(8,128)(2,1)}), bf16[16,8,3584]{2,1,0:T(8,128)(2,1)S(1)}, u32[]{:S(2)}, u32[]{:S(2)}) async-start(bf16[16,8,3584]{2,1,0:T(8,128)(2,1)} %bitcast.57), calls=%async_computation.2 | async-start | bytes 1835008 | tf_op jit(solution)/shard_map/all_to_all | solution.py:53
  118.9 0.0 copy-done.2
  118.9 0.1 copy.18
  118.9 0.1 select_reduce_fusion
  119.0 23.6 %all-to-all-done.1 = bf16[16,8,3584]{2,1,0:T(8,128)(2,1)S(1)} async-done(((bf16[16,8,3584]{2,1,0:T(8,128)(2,1)}), bf16[16,8,3584]{2,1,0:T(8,128)(2,1)S(1)}, u32[]{:S(2)}, u32[]{:S(2)}) %all-to-all-start.1) | async-done | bytes 917536 | tf_op jit(solution)/shard_map/all_to_all | solution.py:53
  142.6 1.1 convolution_convert_fusion.1
  (1 shorter events, 0.0 us)
Async XLA Ops:
  6.5 1.5 %copy-start = (bf16[16,3584]{1,0:T(8,128)(2,1)S(1)}, bf16[16,3584]{1,0:T(8,128)(2,1)}, u32[]{:S(2)}) copy-start(bf16[16,3584]{1,0:T(8,128)(2,1)} %param.6) | copy-start | bytes 344068
  6.5 62.2 %all-gather.2.cloned.1.call-start = ((), (), s32[]{:S(2)}) async-start(), calls=%async_computation.3 | async-start | bytes 2752512 | tf_op jit(solution)/shard_map/all_gather | solution.py:45
  39.5 74.8 %reduce-scatter.2.cloned.1.call-start = ((), (), s32[]{:S(2)}) async-start(), calls=%async_computation.4 | async-start | bytes 2752512 | tf_op jit(solution)/shard_map/reduce_scatter | solution.py:46
  68.7 4.9 %copy-start.1 = (bf16[8,2,2,8,3584]{4,3,1,0,2:T(8,128)(2,1)S(1)}, bf16[8,2,2,8,3584]{4,3,1,0,2:T(8,128)(2,1)}, u32[]{:S(2)}) copy-start(bf16[8,2,2,8,3584]{4,3,1,0,2:T(8,128)(2,1)} %all-gather.2.cloned.1.call-done) | copy-start | bytes 5505028
  82.1 36.7 %copy-start.2 = (f32[16,8]{0,1:T(8,128)S(1)}, f32[16,8]{0,1:T(8,128)}, u32[]{:S(2)}) copy-start(f32[16,8]{0,1:T(8,128)} %param.8) | copy-start | bytes 1540
  114.2 28.4 %all-to-all-start.1 = ((bf16[16,8,3584]{2,1,0:T(8,128)(2,1)}), bf16[16,8,3584]{2,1,0:T(8,128)(2,1)S(1)}, u32[]{:S(2)}, u32[]{:S(2)}) async-start(bf16[16,8,3584]{2,1,0:T(8,128)(2,1)} %bitcast.57), calls=%async_computation.2 | async-start | bytes 1835008 | tf_op jit(solution)/shard_map/all_to_all | solution.py:53
Sparse Core Ops, SparseCore 0:
  39.6 29.0 all-gather.1
  85.3 28.9 reduce-scatter.1
where the time goes:
time: 151 us
  waiting for transfers between devices  81.9 us (54%)
  blocking collectives  29.9 us (20%)
  matrix products  15 us (10%)
  between operations  13.5 us (9%)
  local copies, waits for them, and re-layouts  5.01 us (3%)
  starting transfers between devices  4.66 us (3%)
    all_to_all x1, blocking collectives, shards(): lax.all_to_all(send_buffer, 'expert', split_axis=0, concat_axis=0, tiled=...  29.9 us
    all_gather x1, waiting for transfers between devices, shards(): lax.all_gather(arrived, 'split', axis=1, tiled=True)  29.2 us
    reduce_scatter x1, waiting for transfers between devices, shards(): lax.psum_scatter(partial_value.astype(jnp.float32).astype(jnp.bfloat16),...  29.1 us
    all_to_all x1, waiting for transfers between devices, shards(): lax.all_to_all(expert_out, 'expert', split_axis=0, concat_axis=0, tiled=T...  23.6 us
    dot_general x1, matrix products, run_experts(): jnp.einsum('mjcf,jfd->mjcd', hidden, w_down, preferred_element_type=jnp.f...  8.53 us
    dot_general x1, matrix products, run_experts(): jnp.einsum('mjcd,jdf->mjcf', row_block, w_gate, preferred_element_type=jn...  4.89 us
    all_to_all x1, starting transfers between devices, shards(): lax.all_to_all(expert_out, 'expert', split_axis=0, concat_axis=0, tiled=T...  4.61 us
  transfers between devices with their start and end apart: 3, of which 3 were waited for; matrix products, arithmetic and copies ran while one was open for 0% of the time, Pallas kernels for 0%

commit v1 on v0

--- a/solution.py
+++ b/solution.py
@@ -1,6 +1,8 @@
 import jax
 import jax.numpy as jnp
 from jax import lax
+from jax.experimental import pallas as pl
+from jax.experimental.pallas import tpu as pltpu
 from jax.sharding import PartitionSpec as P
 
 
@@ -61,6 +63,313 @@
     return mixed.astype(jnp.bfloat16)
 
 
+CHUNK = 512
+LANES = 128
+
+
+def fused_kernel(
+    tok_ref, ids_ref, gw_ref, wg_hbm, wu_hbm, wd_hbm, out_ref,
+    xg, ext, wg, wu, wd, acc_g, acc_u, hid, cw, y, s1, r1, s2, r2, s3, r3,
+    wg_sem, wu_sem, wd_sem,
+    ezs, ezr, exs, exr, ecs, ecr,
+    zs, zr, xs, xr, cs, cr,
+    s1s, s1r, s2s, s2r, s3s, s3r,
+):
+    T, width = tok_ref.shape
+    local_count, _, part = wg.shape
+    nz = lax.axis_size("expert") // 2
+    steps = width // CHUNK
+    line = nz * T
+    half = 2 * line
+    e_idx = lax.axis_index("expert")
+    x_idx = lax.axis_index("split")
+    z, core = e_idx // 2, lax.rem(e_idx, 2)
+    core_peer = {"expert": z * 2 + (1 - core), "split": x_idx}
+    x_peer = {"expert": e_idx, "split": 1 - x_idx}
+
+    def z_at(offset):
+        return lax.rem(z + (offset % nz), nz)
+
+    def z_peer(offset):
+        return {"expert": z_at(offset) * 2 + core, "split": x_idx}
+
+    def cols(c):
+        return pl.ds(pl.multiple_of(c * CHUNK, CHUNK), CHUNK)
+
+    def rows(index, base=0):
+        return pl.ds(pl.multiple_of(base + index * T, T), T)
+
+    def remote(src, dst, send, recv, peer):
+        return pltpu.make_async_remote_copy(
+            src_ref=src, dst_ref=dst, send_sem=send, recv_sem=recv,
+            device_id=peer, device_id_type=pl.DeviceIdType.MESH,
+        )
+
+    def w_copy(c):
+        return (
+            pltpu.make_async_copy(wg_hbm.at[:, cols(c), :], wg.at[:, cols(c), :], wg_sem.at[c]),
+            pltpu.make_async_copy(wu_hbm.at[:, cols(c), :], wu.at[:, cols(c), :], wu_sem.at[c]),
+        )
+
+    wd_copy = pltpu.make_async_copy(wd_hbm, wd, wd_sem)
+
+    barrier = pltpu.get_barrier_semaphore()
+    peers = [core_peer, x_peer] + [z_peer(d) for d in range(1, nz)]
+    for peer in peers:
+        pl.semaphore_signal(barrier, inc=1, device_id=peer, device_id_type=pl.DeviceIdType.MESH)
+
+    @pl.loop(0, steps)
+    def _(c):
+        for copy in w_copy(c):
+            copy.start()
+
+    wd_copy.start()
+
+    own = rows(z)
+    xg[own, :] = tok_ref[...]
+    lane = lax.broadcasted_iota(jnp.int32, (T, LANES), 1)
+    table = jnp.zeros((T, LANES), jnp.float32)
+    for k in range(ids_ref.shape[1]):
+        table = table + jnp.where(ids_ref[:, k : k + 1] == lane, gw_ref[:, k : k + 1], 0.0)
+    ext[own, :] = table
+    acc_g[...] = jnp.zeros_like(acc_g)
+    acc_u[...] = jnp.zeros_like(acc_u)
+    pl.semaphore_wait(barrier, len(peers))
+
+    def gz(buf, where, send, recv, d, arriving):
+        block = buf.at[(rows(z_at(-d)) if arriving else own,) + where]
+        return remote(block, block, send.at[d], recv.at[d], z_peer(d))
+
+    def gx(buf, where, send, recv, d, arriving):
+        index = z_at(-d)
+        src = buf.at[(rows(index),) + where]
+        dst = buf.at[(rows(index, line),) + where]
+        if arriving:
+            src = dst
+        return remote(src, dst, send.at[d], recv.at[d], x_peer)
+
+    def gc(buf, where, send, recv, side, arriving):
+        src = buf.at[(pl.ds(side * line, line),) + where]
+        dst = buf.at[(pl.ds(half + side * line, line),) + where]
+        if arriving:
+            src = dst
+        return remote(src, dst, send.at[side], recv.at[side], core_peer)
+
+    e_where = (slice(None),)
+
+    def e_args(send, recv):
+        return ext, e_where, send, recv
+
+    def c_args(c, send, recv):
+        return xg, (cols(c),), send.at[c], recv.at[c]
+
+    def first_sends(za, xa):
+        for d in range(1, nz):
+            gz(*za, d, False).start()
+        gx(*xa, 0, False).start()
+
+    def forward_line(za, xa, ca):
+        for d in range(1, nz):
+            gz(*za, d, True).wait_recv()
+            gx(*xa, d, False).start()
+        gc(*ca, 0, False).start()
+
+    def forward_other(xa, ca):
+        for d in range(nz):
+            gx(*xa, d, True).wait_recv()
+        gc(*ca, 1, False).start()
+
+    def from_core(ca):
+        for side in range(2):
+            gc(*ca, side, True).wait_recv()
+
+    def gather_sent(za, xa, ca):
+        for d in range(1, nz):
+            gz(*za, d, False).wait_send()
+        for d in range(nz):
+            gx(*xa, d, False).wait_send()
+        for side in range(2):
+            gc(*ca, side, False).wait_send()
+
+    ez, ex, ec = e_args(ezs, ezr), e_args(exs, exr), e_args(ecs, ecr)
+    first_sends(ez, ex)
+
+    @pl.loop(0, steps)
+    def _(c):
+        first_sends(c_args(c, zs, zr), c_args(c, xs, xr))
+
+    forward_line(ez, ex, ec)
+
+    @pl.loop(0, steps + 2)
+    def _(i):
+        @pl.when(i < steps)
+        def _():
+            forward_line(c_args(i, zs, zr), c_args(i, xs, xr), c_args(i, cs, cr))
+
+        @pl.when((i >= 1) & (i < steps + 1))
+        def _():
+            forward_other(c_args(i - 1, xs, xr), c_args(i - 1, cs, cr))
+
+        @pl.when(i >= 2)
+        def _():
+            c = i - 2
+            from_core(c_args(c, cs, cr))
+            for copy in w_copy(c):
+                copy.wait()
+            value = xg[:, cols(c)]
+            for j in range(local_count):
+                acc_g[j] += jnp.dot(value, wg[j, cols(c), :], preferred_element_type=jnp.float32)
+                acc_u[j] += jnp.dot(value, wu[j, cols(c), :], preferred_element_type=jnp.float32)
+
+    forward_other(ex, ec)
+    for j in range(local_count):
+        gate = acc_g[j]
+        hid[j] = (gate / (1.0 + jnp.exp(-gate)) * acc_u[j]).astype(jnp.bfloat16)
+    from_core(ec)
+    lanes = lax.broadcasted_iota(jnp.int32, (2 * half, LANES), 1)
+    for j in range(local_count):
+        chosen = jnp.where(lanes == e_idx * local_count + j, ext[...], 0.0)
+        cw[j] = jnp.broadcast_to(jnp.sum(chosen, axis=1, keepdims=True), (2 * half, LANES))
+    wd_copy.wait()
+
+    def rc(c):
+        return remote(s1.at[:, cols(c)], r1.at[:, cols(c)], s1s.at[c], s1r.at[c], core_peer)
+
+    def rx(c):
+        return remote(s2.at[:, cols(c)], r2.at[:, cols(c)], s2s.at[c], s2r.at[c], x_peer)
+
+    def rz(c, d):
+        return remote(
+            s3.at[rows(z_at(d)), cols(c)], r3.at[d, :, cols(c)],
+            s3s.at[c, d], s3r.at[c, d], z_peer(d),
+        )
+
+    lag_x, lag_z, lag_out = 1, 3, 5
+
+    @pl.loop(0, steps + lag_out)
+    def _(i):
+        @pl.when(i < steps)
+        def _():
+            total = None
+            for j in range(local_count):
+                value = jnp.dot(hid[j], wd[j, :, cols(i)], preferred_element_type=jnp.float32)
+                value = value * jnp.concatenate([cw[j]] * (CHUNK // LANES), axis=1)
+                total = value if total is None else total + value
+            s1[:, cols(i)] = total[half:].astype(jnp.bfloat16)
+            y[:, cols(i)] = total[:half]
+            rc(i).start()
+
+        @pl.when((i >= lag_x) & (i < steps + lag_x))
+        def _():
+            c = i - lag_x
+            rc(c).wait_recv()
+            total = y[:, cols(c)] + r1[:, cols(c)].astype(jnp.float32)
+            s2[:, cols(c)] = total[line:].astype(jnp.bfloat16)
+            y[:line, cols(c)] = total[:line]
+            rx(c).start()
+
+        @pl.when((i >= lag_z) & (i < steps + lag_z))
+        def _():
+            c = i - lag_z
+            rx(c).wait_recv()
+            total = y[:line, cols(c)] + r2[:, cols(c)].astype(jnp.float32)
+            s3[:, cols(c)] = total.astype(jnp.bfloat16)
+            y[:line, cols(c)] = total
+            for d in range(1, nz):
+                rz(c, d).start()
+
+        @pl.when(i >= lag_out)
+        def _():
+            c = i - lag_out
+            total = y[own, cols(c)]
+            for d in range(1, nz):
+                rz(c, d).wait_recv()
+                total = total + r3[d, :, cols(c)].astype(jnp.float32)
+            out_ref[:, cols(c)] = total.astype(out_ref.dtype)
+
+    gather_sent(ez, ex, ec)
+
+    @pl.loop(0, steps)
+    def _(c):
+        gather_sent(c_args(c, zs, zr), c_args(c, xs, xr), c_args(c, cs, cr))
+        rc(c).wait_send()
+        rx(c).wait_send()
+        for d in range(1, nz):
+            rz(c, d).wait_send()
+
+
+def fused_shards(tokens, expert_ids, gate_weights, w_gate, w_up, w_down):
+    T, width = tokens.shape
+    local_count, _, part = w_gate.shape
+    nz = lax.axis_size("expert") // 2
+    steps = width // CHUNK
+    line = nz * T
+    half, total = 2 * line, 4 * line
+    bf16, f32 = jnp.bfloat16, jnp.float32
+    dma = pltpu.SemaphoreType.DMA
+    vmem = pl.BlockSpec(memory_space=pltpu.VMEM)
+    hbm = pl.BlockSpec(memory_space=pl.ANY)
+    flops = 2 * total * width * part * local_count * 3
+    return pl.pallas_call(
+        fused_kernel,
+        out_shape=jax.ShapeDtypeStruct((T, width), bf16),
+        in_specs=[vmem] * 3 + [hbm] * 3,
+        out_specs=vmem,
+        scratch_shapes=[
+            pltpu.VMEM((total, width), bf16),
+            pltpu.VMEM((total, LANES), f32),
+            pltpu.VMEM(w_gate.shape, bf16),
+            pltpu.VMEM(w_up.shape, bf16),
+            pltpu.VMEM(w_down.shape, bf16),
+            pltpu.VMEM((local_count, total, part), f32),
+            pltpu.VMEM((local_count, total, part), f32),
+            pltpu.VMEM((local_count, total, part), bf16),
+            pltpu.VMEM((local_count, total, LANES), f32),
+            pltpu.VMEM((half, width), f32),
+            pltpu.VMEM((half, width), bf16),
+            pltpu.VMEM((half, width), bf16),
+            pltpu.VMEM((line, width), bf16),
+            pltpu.VMEM((line, width), bf16),
+            pltpu.VMEM((line, width), bf16),
+            pltpu.VMEM((nz, T, width), bf16),
+            dma((steps,)),
+            dma((steps,)),
+            dma,
+            *[dma((nz,)), dma((nz,)), dma((nz,)), dma((nz,)), dma((2,)), dma((2,))],
+            *[dma((steps, nz))] * 4,
+            *[dma((steps, 2))] * 2,
+            *[dma((steps,))] * 4,
+            *[dma((steps, nz))] * 2,
+        ],
+        compiler_params=pltpu.CompilerParams(
+            collective_id=0, has_side_effects=True, vmem_limit_bytes=50 * 1024 * 1024
+        ),
+        cost_estimate=pl.CostEstimate(
+            flops=flops,
+            bytes_accessed=2 * (w_gate.size + w_up.size + w_down.size),
+            transcendentals=total * part * local_count,
+        ),
+    )(tokens, expert_ids, gate_weights, w_gate, w_up, w_down)
+
+
+def pick(mesh):
+    def body(tokens, expert_ids, gate_weights, w_gate, w_up, w_down):
+        expert_count = mesh.shape["expert"]
+        rows = tokens.shape[0] * expert_count * mesh.shape["split"]
+        fits = (
+            mesh.shape["split"] == 2
+            and expert_count % 2 == 0
+            and rows <= 256
+            and tokens.shape[0] % 16 == 0
+            and tokens.shape[1] % CHUNK == 0
+            and w_gate.shape[0] * expert_count <= LANES
+        )
+        run = fused_shards if fits else shards
+        return run(tokens, expert_ids, gate_weights, w_gate, w_up, w_down)
+
+    return body
+
+
 def solution(mesh):
     in_specs = (
         P(("groups", "expert", "split"), None),
@@ -71,4 +380,4 @@
         P("expert", "split", None),
     )
     out_specs = P(("groups", "expert", "split"), None)
-    return jax.shard_map(shards, mesh=mesh, in_specs=in_specs, out_specs=out_specs, check_vma=False)
+    return jax.shard_map(pick(mesh), mesh=mesh, in_specs=in_specs, out_specs=out_specs, check_vma=False)

time: 151 us -> 52.2 us (0.35)
  waiting for transfers between devices: 81.9 us -> 0 us
  Pallas kernels: 0 us -> 48.9 us
  blocking collectives: 29.9 us -> 0 us
  matrix products: 15 us -> 0 us
  between operations: 13.5 us -> 0.01 us
  starting transfers between devices: 4.66 us -> 0 us
  local copies, waits for them, and re-layouts: 5.01 us -> 3.06 us
    pallas_call x0 -> x1, Pallas kernels: none -> 48.9 us  [fused_shards(): pl.pallas_call(fused_kernel, out_shape=jax.ShapeDtypeStruct((T, width), b...]
    all_to_all x1 -> x0, blocking collectives: 29.9 us -> none  [shards(): lax.all_to_all(send_buffer, 'expert', split_axis=0, concat_axis=0, tiled=...]
    all_gather x1 -> x0, waiting for transfers between devices: 29.2 us -> none  [shards(): lax.all_gather(arrived, 'split', axis=1, tiled=True)]
    reduce_scatter x1 -> x0, waiting for transfers between devices: 29.1 us -> none  [shards(): lax.psum_scatter(partial_value.astype(jnp.float32).astype(jnp.bfloat16),...]
    all_to_all x1 -> x0, waiting for transfers between devices: 23.6 us -> none  [shards(): lax.all_to_all(expert_out, 'expert', split_axis=0, concat_axis=0, tiled=T...]
    dot_general x4 -> x0, matrix products: 15 us -> none  [the longest x1 8.53 us: run_experts(): jnp.einsum('mjcf,jfd->mjcd', hidden, w_down, preferred_element_type=jnp.f...]
    all_to_all x1 -> x0, starting transfers between devices: 4.61 us -> none  [shards(): lax.all_to_all(expert_out, 'expert', split_axis=0, concat_axis=0, tiled=T...]
    reshape x2 -> x0, local copies, waits for them, and re-layouts: 3.97 us -> none  [the longest x1 2.98 us: run_experts(): return partial_value.astype(jnp.bfloat16).reshape(block_shape)]
  transfers between devices with their start and end apart: 3 -> 0, of which waited for: 3 -> 0; matrix products, arithmetic and copies ran while one was open for 0% -> 0% of each run, Pallas kernels for 0% -> 0%
where the time goes in v1:
time: 52.2 us; the launch traced here: 52 us
  Pallas kernels  48.9 us (94%)
  local copies, waits for them, and re-layouts  3.06 us (6%)
    pallas_call x1, Pallas kernels, fused_shards(): pl.pallas_call(fused_kernel, out_shape=jax.ShapeDtypeStruct((T, width), b...  48.9 us
    unnamed x5, local copies, waits for them, and re-layouts  3.06 us

profile of v1, /device:TPU:0, one launch (start us, length us, event | category | flops | bytes accessed | tf_op | source)
XLA Modules:
  0.0 52.0 jit_solution(5059154580189585793)
XLA Ops:
  0.0 0.8 %copy.7.ids_ref = s32[16,8]{1,0:T(8,128)S(1)} copy(s32[16,8]{0,1:T(8,128)} %param.7) | data formatting | bytes 1024 | tf_op args[1]
  0.8 0.8 %copy.8.gw_ref = f32[16,8]{1,0:T(8,128)S(1)} copy(f32[16,8]{0,1:T(8,128)} %param.8) | data formatting | bytes 1024 | tf_op args[2]
  1.5 0.0 copy-start
  1.5 0.9 %copy-done = bf16[16,3584]{1,0:T(8,128)(2,1)S(1)} copy-done((bf16[16,3584]{1,0:T(8,128)(2,1)S(1)}, bf16[16,3584]{1,0:T(8,128)(2,1)}, u32[]{:S(2)}) %copy-start) | copy-done | bytes 114712
  2.4 48.9 %shard_map.64 = bf16[16,3584]{1,0:T(8,128)(2,1)S(1)} custom-call(bf16[16,3584]{1,0:T(8,128)(2,1)S(1)} %copy-done, s32[16,8]{1,0:T(8,128)S(1)} %copy.7.ids_ref, f32[16,8]{1,0:T(8,128)S(1)} %copy.8.gw_ref, bf16[2,3584,512]{2,1,0:T(8,128)(2,1)} %wg_hbm.1, bf16[2,3584,512]{2,1,0:T(8,128)(2,1)} %wu_hbm.1, bf16[2,512,3584]{2,1,0:T(8,128)(2,1)} %wd_hbm.1), custom_call_target="tpu_custom_call" | custom-call | flops 5637144576 | bytes 22020096 | tf_op jit(solution)/shard_map/pallas_call | solution.py:313
  51.3 0.6 %copy.10 = bf16[16,3584]{1,0:T(8,128)(2,1)} copy(bf16[16,3584]{1,0:T(8,128)(2,1)S(1)} %shard_map.64) | data formatting | bytes 229376
Async XLA Ops:
  1.5 0.9 %copy-start = (bf16[16,3584]{1,0:T(8,128)(2,1)S(1)}, bf16[16,3584]{1,0:T(8,128)(2,1)}, u32[]{:S(2)}) copy-start(bf16[16,3584]{1,0:T(8,128)(2,1)} %tok_ref.1) | copy-start | bytes 344068

commit v2 on v1

--- a/solution.py
+++ b/solution.py
@@ -63,22 +63,25 @@
     return mixed.astype(jnp.bfloat16)
 
 
-CHUNK = 512
+GATHER = 896
+REDUCE = 896
+AHEAD = 1
+LAGS = (1, 3, 5)
 LANES = 128
 
 
 def fused_kernel(
-    tok_ref, ids_ref, gw_ref, wg_hbm, wu_hbm, wd_hbm, out_ref,
-    xg, ext, wg, wu, wd, acc_g, acc_u, hid, cw, y, s1, r1, s2, r2, s3, r3,
-    wg_sem, wu_sem, wd_sem,
+    tok_hbm, ids_hbm, gw_hbm, wg_hbm, wu_hbm, wd_hbm, out_ref,
+    xg, ext, ids_ref, gw_ref, wg, wu, wd, acc_g, acc_u, hid, cw, y, s1, r1, s2, r2, s3, r3,
+    tok_sem, ids_sem, gw_sem, wg_sem, wu_sem, wd_sem,
     ezs, ezr, exs, exr, ecs, ecr,
     zs, zr, xs, xr, cs, cr,
     s1s, s1r, s2s, s2r, s3s, s3r,
 ):
-    T, width = tok_ref.shape
+    T, width = tok_hbm.shape
     local_count, _, part = wg.shape
     nz = lax.axis_size("expert") // 2
-    steps = width // CHUNK
+    steps, reduce_steps = width // GATHER, width // REDUCE
     line = nz * T
     half = 2 * line
     e_idx = lax.axis_index("expert")
@@ -93,8 +96,8 @@
     def z_peer(offset):
         return {"expert": z_at(offset) * 2 + core, "split": x_idx}
 
-    def cols(c):
-        return pl.ds(pl.multiple_of(c * CHUNK, CHUNK), CHUNK)
+    def cols(c, size=GATHER):
+        return pl.ds(pl.multiple_of(c * size, size), size)
 
     def rows(index, base=0):
         return pl.ds(pl.multiple_of(base + index * T, T), T)
@@ -105,6 +108,13 @@
             device_id=peer, device_id_type=pl.DeviceIdType.MESH,
         )
 
+    own = rows(z)
+    tok_copy = pltpu.make_async_copy(tok_hbm, xg.at[own, :], tok_sem)
+    ids_copy = pltpu.make_async_copy(ids_hbm, ids_ref, ids_sem)
+    gw_copy = pltpu.make_async_copy(gw_hbm, gw_ref, gw_sem)
+    for copy in (ids_copy, gw_copy, tok_copy):
+        copy.start()
+
     def w_copy(c):
         return (
             pltpu.make_async_copy(wg_hbm.at[:, cols(c), :], wg.at[:, cols(c), :], wg_sem.at[c]),
@@ -125,15 +135,17 @@
 
     wd_copy.start()
 
-    own = rows(z)
-    xg[own, :] = tok_ref[...]
+    acc_g[...] = jnp.zeros_like(acc_g)
+    acc_u[...] = jnp.zeros_like(acc_u)
+    ids_copy.wait()
+    gw_copy.wait()
+    ids, weights = jnp.transpose(ids_ref[...]), jnp.transpose(gw_ref[...])
     lane = lax.broadcasted_iota(jnp.int32, (T, LANES), 1)
     table = jnp.zeros((T, LANES), jnp.float32)
-    for k in range(ids_ref.shape[1]):
-        table = table + jnp.where(ids_ref[:, k : k + 1] == lane, gw_ref[:, k : k + 1], 0.0)
+    for k in range(ids.shape[1]):
+        table = table + jnp.where(ids[:, k : k + 1] == lane, weights[:, k : k + 1], 0.0)
     ext[own, :] = table
-    acc_g[...] = jnp.zeros_like(acc_g)
-    acc_u[...] = jnp.zeros_like(acc_u)
+    tok_copy.wait()
     pl.semaphore_wait(barrier, len(peers))
 
     def gz(buf, where, send, recv, d, arriving):
@@ -194,14 +206,16 @@
     ez, ex, ec = e_args(ezs, ezr), e_args(exs, exr), e_args(ecs, ecr)
     first_sends(ez, ex)
 
-    @pl.loop(0, steps)
-    def _(c):
+    for c in range(AHEAD):
         first_sends(c_args(c, zs, zr), c_args(c, xs, xr))
-
     forward_line(ez, ex, ec)
 
     @pl.loop(0, steps + 2)
     def _(i):
+        @pl.when(i + AHEAD < steps)
+        def _():
+            first_sends(c_args(i + AHEAD, zs, zr), c_args(i + AHEAD, xs, xr))
+
         @pl.when(i < steps)
         def _():
             forward_line(c_args(i, zs, zr), c_args(i, xs, xr), c_args(i, cs, cr))
@@ -209,6 +223,19 @@
         @pl.when((i >= 1) & (i < steps + 1))
         def _():
             forward_other(c_args(i - 1, xs, xr), c_args(i - 1, cs, cr))
+
+        @pl.when(i == 1)
+        def _():
+            forward_other(ex, ec)
+
+        @pl.when(i == 2)
+        def _():
+            from_core(ec)
+            lanes = lax.broadcasted_iota(jnp.int32, (2 * half, LANES), 1)
+            for j in range(local_count):
+                chosen = jnp.where(lanes == e_idx * local_count + j, ext[...], 0.0)
+                weight = jnp.sum(chosen, axis=1, keepdims=True)
+                cw[j] = jnp.broadcast_to(weight, (2 * half, LANES))
 
         @pl.when(i >= 2)
         def _():
@@ -221,88 +248,82 @@
                 acc_g[j] += jnp.dot(value, wg[j, cols(c), :], preferred_element_type=jnp.float32)
                 acc_u[j] += jnp.dot(value, wu[j, cols(c), :], preferred_element_type=jnp.float32)
 
-    forward_other(ex, ec)
     for j in range(local_count):
         gate = acc_g[j]
         hid[j] = (gate / (1.0 + jnp.exp(-gate)) * acc_u[j]).astype(jnp.bfloat16)
-    from_core(ec)
-    lanes = lax.broadcasted_iota(jnp.int32, (2 * half, LANES), 1)
-    for j in range(local_count):
-        chosen = jnp.where(lanes == e_idx * local_count + j, ext[...], 0.0)
-        cw[j] = jnp.broadcast_to(jnp.sum(chosen, axis=1, keepdims=True), (2 * half, LANES))
     wd_copy.wait()
 
     def rc(c):
-        return remote(s1.at[:, cols(c)], r1.at[:, cols(c)], s1s.at[c], s1r.at[c], core_peer)
+        return remote(s1.at[:, cols(c, REDUCE)], r1.at[:, cols(c, REDUCE)], s1s.at[c], s1r.at[c], core_peer)
 
     def rx(c):
-        return remote(s2.at[:, cols(c)], r2.at[:, cols(c)], s2s.at[c], s2r.at[c], x_peer)
+        return remote(s2.at[:, cols(c, REDUCE)], r2.at[:, cols(c, REDUCE)], s2s.at[c], s2r.at[c], x_peer)
 
     def rz(c, d):
         return remote(
-            s3.at[rows(z_at(d)), cols(c)], r3.at[d, :, cols(c)],
+            s3.at[rows(z_at(d)), cols(c, REDUCE)], r3.at[d, :, cols(c, REDUCE)],
             s3s.at[c, d], s3r.at[c, d], z_peer(d),
         )
 
-    lag_x, lag_z, lag_out = 1, 3, 5
-
-    @pl.loop(0, steps + lag_out)
+    lag_x, lag_z, lag_out = LAGS
+
+    @pl.loop(0, reduce_steps + lag_out)
     def _(i):
-        @pl.when(i < steps)
+        @pl.when(i < reduce_steps)
         def _():
             total = None
             for j in range(local_count):
-                value = jnp.dot(hid[j], wd[j, :, cols(i)], preferred_element_type=jnp.float32)
-                value = value * jnp.concatenate([cw[j]] * (CHUNK // LANES), axis=1)
+                value = jnp.dot(hid[j], wd[j, :, cols(i, REDUCE)], preferred_element_type=jnp.float32)
+                value = value * jnp.concatenate([cw[j]] * (REDUCE // LANES), axis=1)
                 total = value if total is None else total + value
-            s1[:, cols(i)] = total[half:].astype(jnp.bfloat16)
-            y[:, cols(i)] = total[:half]
+            s1[:, cols(i, REDUCE)] = total[half:].astype(jnp.bfloat16)
+            y[:, cols(i, REDUCE)] = total[:half]
             rc(i).start()
 
-        @pl.when((i >= lag_x) & (i < steps + lag_x))
+        @pl.when((i >= lag_x) & (i < reduce_steps + lag_x))
         def _():
             c = i - lag_x
             rc(c).wait_recv()
-            total = y[:, cols(c)] + r1[:, cols(c)].astype(jnp.float32)
-            s2[:, cols(c)] = total[line:].astype(jnp.bfloat16)
-            y[:line, cols(c)] = total[:line]
+            total = y[:, cols(c, REDUCE)] + r1[:, cols(c, REDUCE)].astype(jnp.float32)
+            s2[:, cols(c, REDUCE)] = total[line:].astype(jnp.bfloat16)
+            y[:line, cols(c, REDUCE)] = total[:line]
             rx(c).start()
 
-        @pl.when((i >= lag_z) & (i < steps + lag_z))
+        @pl.when((i >= lag_z) & (i < reduce_steps + lag_z))
         def _():
             c = i - lag_z
             rx(c).wait_recv()
-            total = y[:line, cols(c)] + r2[:, cols(c)].astype(jnp.float32)
-            s3[:, cols(c)] = total.astype(jnp.bfloat16)
-            y[:line, cols(c)] = total
+            total = y[:line, cols(c, REDUCE)] + r2[:, cols(c, REDUCE)].astype(jnp.float32)
+            s3[:, cols(c, REDUCE)] = total.astype(jnp.bfloat16)
+            y[:line, cols(c, REDUCE)] = total
             for d in range(1, nz):
                 rz(c, d).start()
 
         @pl.when(i >= lag_out)
         def _():
             c = i - lag_out
-            total = y[own, cols(c)]
+            total = y[own, cols(c, REDUCE)]
             for d in range(1, nz):
                 rz(c, d).wait_recv()
-                total = total + r3[d, :, cols(c)].astype(jnp.float32)
-            out_ref[:, cols(c)] = total.astype(out_ref.dtype)
+                total = total + r3[d, :, cols(c, REDUCE)].astype(jnp.float32)
+            out_ref[:, cols(c, REDUCE)] = total.astype(out_ref.dtype)
+            rc(c).wait_send()
+            rx(c).wait_send()
+            for d in range(1, nz):
+                rz(c, d).wait_send()
+
+        @pl.when(i < steps)
+        def _():
+            gather_sent(c_args(i, zs, zr), c_args(i, xs, xr), c_args(i, cs, cr))
 
     gather_sent(ez, ex, ec)
-
-    @pl.loop(0, steps)
-    def _(c):
-        gather_sent(c_args(c, zs, zr), c_args(c, xs, xr), c_args(c, cs, cr))
-        rc(c).wait_send()
-        rx(c).wait_send()
-        for d in range(1, nz):
-            rz(c, d).wait_send()
 
 
 def fused_shards(tokens, expert_ids, gate_weights, w_gate, w_up, w_down):
     T, width = tokens.shape
     local_count, _, part = w_gate.shape
     nz = lax.axis_size("expert") // 2
-    steps = width // CHUNK
+    steps, reduce_steps = width // GATHER, width // REDUCE
     line = nz * T
     half, total = 2 * line, 4 * line
     bf16, f32 = jnp.bfloat16, jnp.float32
@@ -313,11 +334,13 @@
     return pl.pallas_call(
         fused_kernel,
         out_shape=jax.ShapeDtypeStruct((T, width), bf16),
-        in_specs=[vmem] * 3 + [hbm] * 3,
+        in_specs=[hbm] * 6,
         out_specs=vmem,
         scratch_shapes=[
             pltpu.VMEM((total, width), bf16),
             pltpu.VMEM((total, LANES), f32),
+            pltpu.VMEM((expert_ids.shape[1], T), jnp.int32),
+            pltpu.VMEM((expert_ids.shape[1], T), f32),
             pltpu.VMEM(w_gate.shape, bf16),
             pltpu.VMEM(w_up.shape, bf16),
             pltpu.VMEM(w_down.shape, bf16),
@@ -332,14 +355,15 @@
             pltpu.VMEM((line, width), bf16),
             pltpu.VMEM((line, width), bf16),
             pltpu.VMEM((nz, T, width), bf16),
+            *[dma] * 3,
             dma((steps,)),
             dma((steps,)),
             dma,
             *[dma((nz,)), dma((nz,)), dma((nz,)), dma((nz,)), dma((2,)), dma((2,))],
             *[dma((steps, nz))] * 4,
             *[dma((steps, 2))] * 2,
-            *[dma((steps,))] * 4,
-            *[dma((steps, nz))] * 2,
+            *[dma((reduce_steps,))] * 4,
+            *[dma((reduce_steps, nz))] * 2,
         ],
         compiler_params=pltpu.CompilerParams(
             collective_id=0, has_side_effects=True, vmem_limit_bytes=50 * 1024 * 1024
@@ -349,7 +373,7 @@
             bytes_accessed=2 * (w_gate.size + w_up.size + w_down.size),
             transcendentals=total * part * local_count,
         ),
-    )(tokens, expert_ids, gate_weights, w_gate, w_up, w_down)
+    )(tokens, expert_ids.T, gate_weights.T, w_gate, w_up, w_down)
 
 
 def pick(mesh):
@@ -361,7 +385,8 @@
             and expert_count % 2 == 0
             and rows <= 256
             and tokens.shape[0] % 16 == 0
-            and tokens.shape[1] % CHUNK == 0
+            and tokens.shape[1] % GATHER == 0
+            and tokens.shape[1] % REDUCE == 0
             and w_gate.shape[0] * expert_count <= LANES
         )
         run = fused_shards if fits else shards

time: 52.2 us -> 49.1 us (0.941)
  Pallas kernels: 48.9 us -> 45.9 us
    pallas_call x1, Pallas kernels: 48.9 us -> 45.9 us  [fused_shards(): pl.pallas_call(fused_kernel, out_shape=jax.ShapeDtypeStruct((T, width), b...]
    unnamed x5 -> x7, local copies, waits for them, and re-layouts: 3.06 us -> 2.92 us
where the time goes in v2:
time: 49.1 us; the launch traced here: 48.8 us
  Pallas kernels  45.9 us (93%)
  local copies, waits for them, and re-layouts  2.92 us (6%)
    pallas_call x1, Pallas kernels, fused_shards(): pl.pallas_call(fused_kernel, out_shape=jax.ShapeDtypeStruct((T, width), b...  45.9 us
    unnamed x7, local copies, waits for them, and re-layouts  2.92 us

profile of v2, /device:TPU:0, one launch (start us, length us, event | category | flops | bytes accessed | tf_op | source)
XLA Modules:
  0.0 48.8 jit_solution(2583061765890578268)
XLA Ops:
  0.0 0.0 copy-start
  0.0 0.9 %copy-done = bf16[16,3584]{1,0:T(8,128)(2,1)S(1)} copy-done((bf16[16,3584]{1,0:T(8,128)(2,1)S(1)}, bf16[16,3584]{1,0:T(8,128)(2,1)}, u32[]{:S(2)}) %copy-start) | copy-done | bytes 114712
  0.9 0.0 copy-start.1
  0.9 0.7 %copy-done.1 = s32[16,8]{0,1:T(8,128)S(1)} copy-done((s32[16,8]{0,1:T(8,128)S(1)}, s32[16,8]{0,1:T(8,128)}, u32[]{:S(2)}) %copy-start.1) | copy-done | bytes 536
  1.6 0.0 copy-start.2
  1.6 0.7 %copy-done.2 = f32[16,8]{0,1:T(8,128)S(1)} copy-done((f32[16,8]{0,1:T(8,128)S(1)}, f32[16,8]{0,1:T(8,128)}, u32[]{:S(2)}) %copy-start.2) | copy-done | bytes 536
  2.3 45.9 %shard_map.64 = bf16[16,3584]{1,0:T(8,128)(2,1)S(1)} custom-call(bf16[16,3584]{1,0:T(8,128)(2,1)S(1)} %copy-done, s32[8,16]{1,0:T(8,128)S(1)} %bitcast.2, f32[8,16]{1,0:T(8,128)S(1)} %bitcast.3, bf16[2,3584,512]{2,1,0:T(8,128)(2,1)} %wg_hbm.1, bf16[2,3584,512]{2,1,0:T(8,128)(2,1)} %wu_hbm.1, bf16[2,512,3584]{2,1,0:T(8,128)(2,1)} %wd_hbm.1), custom_call_target="tpu_custom_call" | custom-call | flops 5637144576 | bytes 22020096 | tf_op jit(solution)/shard_map/pallas_call | solution.py:334
  48.2 0.6 %copy.8 = bf16[16,3584]{1,0:T(8,128)(2,1)} copy(bf16[16,3584]{1,0:T(8,128)(2,1)S(1)} %shard_map.64) | data formatting | bytes 229376
Async XLA Ops:
  0.0 0.9 %copy-start = (bf16[16,3584]{1,0:T(8,128)(2,1)S(1)}, bf16[16,3584]{1,0:T(8,128)(2,1)}, u32[]{:S(2)}) copy-start(bf16[16,3584]{1,0:T(8,128)(2,1)} %tok_hbm.1) | copy-start | bytes 344068
  0.9 0.7 %copy-start.1 = (s32[16,8]{0,1:T(8,128)S(1)}, s32[16,8]{0,1:T(8,128)}, u32[]{:S(2)}) copy-start(s32[16,8]{0,1:T(8,128)} %param.7) | copy-start | bytes 1540
  1.6 0.7 %copy-start.2 = (f32[16,8]{0,1:T(8,128)S(1)}, f32[16,8]{0,1:T(8,128)}, u32[]{:S(2)}) copy-start(f32[16,8]{0,1:T(8,128)} %param.8) | copy-start | bytes 1540

commit v3 on v2

--- a/solution.py
+++ b/solution.py
@@ -66,7 +66,7 @@
 GATHER = 896
 REDUCE = 896
 AHEAD = 1
-LAGS = (1, 3, 5)
+LAGS = (1, 2, 4)
 LANES = 128
 
 
@@ -175,13 +175,15 @@
     def c_args(c, send, recv):
         return xg, (cols(c),), send.at[c], recv.at[c]
 
+    near_first = sorted(range(1, nz), key=lambda d: min(d, nz - d))
+
     def first_sends(za, xa):
-        for d in range(1, nz):
+        gx(*xa, 0, False).start()
+        for d in near_first:
             gz(*za, d, False).start()
-        gx(*xa, 0, False).start()
 
     def forward_line(za, xa, ca):
-        for d in range(1, nz):
+        for d in near_first:
             gz(*za, d, True).wait_recv()
             gx(*xa, d, False).start()
         gc(*ca, 0, False).start()

time: 49.1 us -> 47.8 us (0.974)
  Pallas kernels: 45.9 us -> 44.6 us
    pallas_call x1, Pallas kernels: 45.9 us -> 44.6 us  [fused_shards(): pl.pallas_call(fused_kernel, out_shape=jax.ShapeDtypeStruct((T, width), b...]
where the time goes in v3:
time: 47.8 us; the launch traced here: 47.6 us
  Pallas kernels  44.6 us (93%)
  local copies, waits for them, and re-layouts  2.92 us (6%)
    pallas_call x1, Pallas kernels, fused_shards(): pl.pallas_call(fused_kernel, out_shape=jax.ShapeDtypeStruct((T, width), b...  44.6 us
    unnamed x7, local copies, waits for them, and re-layouts  2.92 us

profile of v3, /device:TPU:0, one launch (start us, length us, event | category | flops | bytes accessed | tf_op | source)
XLA Modules:
  0.0 47.6 jit_solution(11367470111242499480)
XLA Ops:
  0.0 0.0 copy-start
  0.0 0.9 %copy-done = bf16[16,3584]{1,0:T(8,128)(2,1)S(1)} copy-done((bf16[16,3584]{1,0:T(8,128)(2,1)S(1)}, bf16[16,3584]{1,0:T(8,128)(2,1)}, u32[]{:S(2)}) %copy-start) | copy-done | bytes 114712
  0.9 0.0 copy-start.1
  0.9 0.7 %copy-done.1 = s32[16,8]{0,1:T(8,128)S(1)} copy-done((s32[16,8]{0,1:T(8,128)S(1)}, s32[16,8]{0,1:T(8,128)}, u32[]{:S(2)}) %copy-start.1) | copy-done | bytes 536
  1.6 0.0 copy-start.2
  1.6 0.7 %copy-done.2 = f32[16,8]{0,1:T(8,128)S(1)} copy-done((f32[16,8]{0,1:T(8,128)S(1)}, f32[16,8]{0,1:T(8,128)}, u32[]{:S(2)}) %copy-start.2) | copy-done | bytes 536
  2.3 44.6 %shard_map.64 = bf16[16,3584]{1,0:T(8,128)(2,1)S(1)} custom-call(bf16[16,3584]{1,0:T(8,128)(2,1)S(1)} %copy-done, s32[8,16]{1,0:T(8,128)S(1)} %bitcast.2, f32[8,16]{1,0:T(8,128)S(1)} %bitcast.3, bf16[2,3584,512]{2,1,0:T(8,128)(2,1)} %wg_hbm.1, bf16[2,3584,512]{2,1,0:T(8,128)(2,1)} %wu_hbm.1, bf16[2,512,3584]{2,1,0:T(8,128)(2,1)} %wd_hbm.1), custom_call_target="tpu_custom_call" | custom-call | flops 5637144576 | bytes 22020096 | tf_op jit(solution)/shard_map/pallas_call | solution.py:336
  46.9 0.6 %copy.8 = bf16[16,3584]{1,0:T(8,128)(2,1)} copy(bf16[16,3584]{1,0:T(8,128)(2,1)S(1)} %shard_map.64) | data formatting | bytes 229376
Async XLA Ops:
  0.0 0.9 %copy-start = (bf16[16,3584]{1,0:T(8,128)(2,1)S(1)}, bf16[16,3584]{1,0:T(8,128)(2,1)}, u32[]{:S(2)}) copy-start(bf16[16,3584]{1,0:T(8,128)(2,1)} %tok_hbm.1) | copy-start | bytes 344068
  0.9 0.7 %copy-start.1 = (s32[16,8]{0,1:T(8,128)S(1)}, s32[16,8]{0,1:T(8,128)}, u32[]{:S(2)}) copy-start(s32[16,8]{0,1:T(8,128)} %param.7) | copy-start | bytes 1540
  1.6 0.7 %copy-start.2 = (f32[16,8]{0,1:T(8,128)S(1)}, f32[16,8]{0,1:T(8,128)}, u32[]{:S(2)}) copy-start(f32[16,8]{0,1:T(8,128)} %param.8) | copy-start | bytes 1540
